TPU v7x, 512 devices: a whole 4x4x16 slice. The times are simulated.
512 devices in a mesh: dp: 4 (over x), seq: 32 (over z, core), head: 4 (over y).
Axes of the slice: x: 4, y: 4, z: 16, core: 2. Of those that a mesh axis runs over, the one named last changes fastest.
Arguments:
- txt_qkv: bfloat16 [32, 256, 3, 2048], P('dp', 'seq', None, 'head'), may hold values from -6 to 6
- img_qkv: bfloat16 [32, 1792, 3, 2048], P('dp', 'seq', None, 'head'), may hold values from -6 to 6
- txt_grad_out: bfloat16 [32, 256, 2048], P('dp', 'seq', 'head'), may hold values from -6 to 6
- img_grad_out: bfloat16 [32, 1792, 2048], P('dp', 'seq', 'head'), may hold values from -6 to 6
- caption_len: int32 [32], P('dp'), may hold values from 1 to 256, as said below
- norm_gains: float32 [4, 128], replicated, may hold values from 0.5 to 6
Outputs:
- txt_out: bfloat16 [32, 256, 2048], P('dp', 'seq', 'head')
- img_out: bfloat16 [32, 1792, 2048], P('dp', 'seq', 'head')
- txt_grads: bfloat16 [32, 256, 3, 2048], P('dp', 'seq', None, 'head')
- img_grads: bfloat16 [32, 1792, 3, 2048], P('dp', 'seq', None, 'head')
- gain_grad: float32 [4, 128], replicated
Inputs may be any that keep to these rules, and one draw needn't show every extreme that they name: `caption_len`: caption slots from a sample's length on are padding; in every draw some sample fills all 256 slots.
All inputs are finite; a program needn't handle non-finite values.
Results may differ from a plain program's by a relative error of at most 0.029.
The roundings to bfloat16 on the way count: a program that leaves them out, or rounds other values in their place, can miss the bound.
Values may be sent and summed in bfloat16 or wider, within the bound.
A program may use at most 64 MiB of HBM per device.

v0:
```python
import math

import jax
import jax.numpy as jnp
from jax import lax
from jax.sharding import PartitionSpec as P

EPSILON = 1e-06


def rms_forward(raw_part, text_rows, gain_text, gain_image, dhead):
    raw_values = raw_part.astype(jnp.float32).reshape(raw_part.shape[0], -1, dhead)
    inverse = lax.rsqrt(jnp.mean(raw_values * raw_values, axis=-1) + EPSILON)
    normed = raw_values * inverse[..., None]
    row_gain = jnp.where(text_rows[:, None], gain_text[None, :], gain_image[None, :])
    scaled = (normed * row_gain[:, None, :]).astype(jnp.bfloat16)
    return (normed, inverse, row_gain, scaled)


def rms_backward(grad_scaled, normed, inverse, row_gain, text_rows):
    grad_values = grad_scaled.astype(jnp.float32)
    grad_normed = grad_values * row_gain[:, None, :]
    inner = jnp.mean(grad_normed * normed, axis=-1, keepdims=True)
    grad_raw = (inverse[..., None] * (grad_normed - normed * inner)).astype(jnp.bfloat16)
    per_row = jnp.sum(grad_values * normed, axis=1)
    text_part = jnp.sum(jnp.where(text_rows[:, None], per_row, 0.0), axis=0)
    image_part = jnp.sum(jnp.where(text_rows[:, None], 0.0, per_row), axis=0)
    return (grad_raw, text_part, image_part)


def shards(txt_qkv, img_qkv, txt_grad_out, img_grad_out, caption_len, norm_gains):
    seq_count = lax.axis_size("seq")
    samples = txt_qkv.shape[0]
    groups = seq_count // samples
    dhead = norm_gains.shape[1]
    text_block = txt_qkv.shape[1]
    block_rows = text_block + img_qkv.shape[1]
    full_width = txt_qkv.shape[3]
    part_width = full_width // groups
    local_heads = part_width // dhead
    score_scale = 1.0 / math.sqrt(dhead)
    text_home = jnp.concatenate([txt_qkv, txt_grad_out[:, :, None, :]], axis=2)
    image_home = jnp.concatenate([img_qkv, img_grad_out[:, :, None, :]], axis=2)
    home = jnp.concatenate([text_home, image_home], axis=1)
    outgoing = home.reshape(samples, block_rows, 4, groups, part_width).transpose(0, 3, 1, 2, 4)
    outgoing = outgoing.reshape(seq_count, block_rows, 4, part_width)
    arrived = lax.all_to_all(outgoing, "seq", split_axis=0, concat_axis=0, tiled=True)
    row_count = seq_count * block_rows
    joint = arrived.reshape(row_count, 4, part_width)
    places = jnp.arange(row_count, dtype=jnp.int32)
    within = places % block_rows
    source = places // block_rows
    is_text = within < text_block
    sample_index = lax.axis_index("seq") // groups
    length = lax.dynamic_index_in_dim(caption_len, sample_index, keepdims=False)
    live = jnp.where(is_text, source * text_block + within < length, True)
    q_side = rms_forward(joint[:, 0], is_text, norm_gains[2], norm_gains[0], dhead)
    k_side = rms_forward(joint[:, 1], is_text, norm_gains[3], norm_gains[1], dhead)
    query_heads = q_side[3]
    key_heads = k_side[3]
    value_heads = joint[:, 2].reshape(row_count, local_heads, dhead)
    cot_heads = joint[:, 3].reshape(row_count, local_heads, dhead)
    tile = math.gcd(row_count, 512)
    tiles = row_count // tile

    def one_block(carry, index):
        key_total, value_total = carry
        start = index * tile
        query_block = lax.dynamic_slice_in_dim(query_heads, start, tile, 0)
        cot_block = lax.dynamic_slice_in_dim(cot_heads, start, tile, 0)
        scores = (
            jnp.einsum("qhd,khd->hqk", query_block, key_heads, preferred_element_type=jnp.float32)
            * score_scale
        )
        masked = jnp.where(live[None, None, :], scores, -jnp.inf)
        peak = jnp.max(masked, axis=-1, keepdims=True)
        totals = jnp.sum(jnp.exp(masked - peak), axis=-1, keepdims=True)
        log_total = peak + jnp.log(totals)
        weights = jnp.where(live[None, None, :], jnp.exp(scores - log_total), 0.0)
        weights_low = weights.astype(jnp.bfloat16)
        attended = jnp.einsum(
            "hqk,khd->qhd", weights_low, value_heads, preferred_element_type=jnp.float32
        ).astype(jnp.bfloat16)
        row_delta = jnp.sum(
            cot_block.astype(jnp.float32) * attended.astype(jnp.float32), axis=-1
        ).T[..., None]
        grad_weights = jnp.einsum(
            "qhd,khd->hqk", cot_block, value_heads, preferred_element_type=jnp.float32
        )
        grad_scores = (weights * (grad_weights - row_delta)).astype(jnp.bfloat16)
        grad_query = (
            jnp.einsum("hqk,khd->qhd", grad_scores, key_heads, preferred_element_type=jnp.float32)
            * score_scale
        ).astype(jnp.bfloat16)
        key_total = key_total + jnp.einsum(
            "hqk,qhd->khd", grad_scores, query_block, preferred_element_type=jnp.float32
        )
        value_total = value_total + jnp.einsum(
            "hqk,qhd->khd", weights_low, cot_block, preferred_element_type=jnp.float32
        )
        return ((key_total, value_total), (attended, grad_query))

    empty = jnp.zeros((row_count, local_heads, dhead), jnp.float32)
    sums, per_block = lax.scan(one_block, (empty, empty), jnp.arange(tiles, dtype=jnp.int32))
    attended = per_block[0].reshape(row_count, local_heads, dhead)
    grad_query = per_block[1].reshape(row_count, local_heads, dhead)
    grad_key = (sums[0] * score_scale).astype(jnp.bfloat16)
    grad_value = sums[1].astype(jnp.bfloat16)
    grad_q_raw, q_text, q_image = rms_backward(grad_query, q_side[0], q_side[1], q_side[2], is_text)
    grad_k_raw, k_text, k_image = rms_backward(grad_key, k_side[0], k_side[1], k_side[2], is_text)
    sending = jnp.stack(
        [
            grad_q_raw.reshape(row_count, part_width),
            grad_k_raw.reshape(row_count, part_width),
            grad_value.reshape(row_count, part_width),
            attended.reshape(row_count, part_width),
        ],
        axis=1,
    )
    back = lax.all_to_all(
        sending.reshape(seq_count, block_rows, 4, part_width),
        "seq",
        split_axis=0,
        concat_axis=0,
        tiled=True,
    )
    returned = back.reshape(samples, groups, block_rows, 4, part_width).transpose(0, 2, 3, 1, 4)
    returned = returned.reshape(samples, block_rows, 4, full_width)
    grads = returned[:, :, :3]
    gain_grad = lax.psum(jnp.stack([q_image, k_image, q_text, k_text]), ("dp", "seq", "head"))
    return (
        returned[:, :text_block, 3],
        returned[:, text_block:, 3],
        grads[:, :text_block],
        grads[:, text_block:],
        gain_grad,
    )


def solution(mesh):
    placed = (
        P("dp", "seq", None, "head"),
        P("dp", "seq", None, "head"),
        P("dp", "seq", "head"),
        P("dp", "seq", "head"),
        P("dp"),
        P(),
    )
    return jax.shard_map(
        shards,
        mesh=mesh,
        in_specs=placed,
        out_specs=(
            P("dp", "seq", "head"),
            P("dp", "seq", "head"),
            P("dp", "seq", None, "head"),
            P("dp", "seq", None, "head"),
            P(),
        ),
        check_vma=False,
    )
```

profile of v0, /device:TPU:1, one launch (start us, length us, event | category | flops | bytes accessed | tf_op | source)
XLA Modules:
  0.0 368.8 jit_solution(2582404996756493627)
XLA Ops:
  0.6 1.7 maximum_maximum_fusion
  2.4 0.6 fusion.56
  3.2 1.6 copy.38
  4.7 16.8 %all-to-all-start = ((bf16[32,64,4,128]{3,1,2,0:T(8,128)(2,1)}), bf16[32,64,4,128]{3,1,2,0:T(8,128)(2,1)}, u32[]{:S(2)}, u32[]{:S(2)}) async-start(bf16[32,64,4,128]{3,1,2,0:T(8,128)(2,1)} %copy.38), calls=%async_computation | async-start | bytes 4194304 | tf_op jit(solution)/shard_map/all_to_all | solution.py:47
  21.6 0.7 dynamic_slice.14
  22.4 97.8 %all-to-all-done = bf16[32,64,4,128]{3,1,2,0:T(8,128)(2,1)} async-done(((bf16[32,64,4,128]{3,1,2,0:T(8,128)(2,1)}), bf16[32,64,4,128]{3,1,2,0:T(8,128)(2,1)}, u32[]{:S(2)}, u32[]{:S(2)}) %all-to-all-start) | async-done | bytes 2097184 | tf_op jit(solution)/shard_map/all_to_all | solution.py:47
  120.2 1.8 copy.39
  122.0 0.6 fusion.46
  122.6 1.1 fusion.55
  123.7 1.6 fusion.50
  125.4 56.6 %while.17 = (s32[]{:T(128)}, f32[2048,1,128]{0,2,1:T(8,128)S(1)}, f32[2048,1,128]{0,2,1:T(8,128)S(1)}, bf16[4,512,1,128]{3,1,0,2:T(8,128)(2,1)}, bf16[4,512,1,12...) while((s32[]{:T(128)}, f32[2048,1,128]{0,2,1:T(8,128)S(1)}, ...), condition=%wide.region_6.7_spmd.clone, body=%wide.region_2.6_spmd.clone.sunk | while | flops 1634173952 | bytes 73312824 | solution.py:104
  125.4 0.6 dynamic_slice.36
  126.7 0.6 fusion.81
  127.3 0.9 constant_dynamic-slice_fusion.2
  128.4 0.8 select_reduce_fusion.6
  129.2 0.9 exponential_reduce_fusion.2
  130.2 1.6 multiply_reduce_fusion.2
  131.9 0.7 constant_dynamic-update-slice_fusion.2
  132.6 3.6 fusion.83
  136.3 1.3 multiply_convert_fusion.4
  137.6 1.4 fusion.84
  139.0 0.5 fusion.82
  139.6 0.6 dynamic_slice.36
  140.8 0.6 fusion.81
  141.4 0.9 constant_dynamic-slice_fusion.2
  142.5 0.8 select_reduce_fusion.6
  143.3 0.9 exponential_reduce_fusion.2
  144.3 1.6 multiply_reduce_fusion.2
  146.1 0.7 constant_dynamic-update-slice_fusion.2
  146.8 3.6 fusion.83
  150.4 1.3 multiply_convert_fusion.4
  151.7 1.4 fusion.84
  153.7 0.6 dynamic_slice.36
  155.0 0.6 fusion.81
  155.6 0.9 constant_dynamic-slice_fusion.2
  156.6 0.8 select_reduce_fusion.6
  157.5 0.9 exponential_reduce_fusion.2
  158.4 1.6 multiply_reduce_fusion.2
  160.2 0.7 constant_dynamic-update-slice_fusion.2
  160.9 3.7 fusion.83
  164.6 1.3 multiply_convert_fusion.4
  165.9 1.4 fusion.84
  167.9 0.6 dynamic_slice.36
  169.1 0.6 fusion.81
  169.8 0.9 constant_dynamic-slice_fusion.2
  170.8 0.8 select_reduce_fusion.6
  171.7 0.9 exponential_reduce_fusion.2
  172.6 1.6 multiply_reduce_fusion.2
  174.4 0.7 constant_dynamic-update-slice_fusion.2
  175.1 3.6 fusion.83
  178.7 1.3 multiply_convert_fusion.4
  180.0 1.4 fusion.84
  182.0 1.0 copy.43
  183.1 1.3 copy.42
  184.4 4.1 %select_reduce_fusion.4 = (f32[128]{0:T(128)S(1)}, f32[128]{0:T(128)S(1)}, f32[128]{0:T(128)S(1)}, f32[128]{0:T(128)S(1)}, bf16[2048,1,128]{2,0,1:T(8,128)(2,1)S(1)}) fusion(bf16[2048,1,128]{2,0,1:T(8,128)(2,1)} %bitcast.151, f32[2048]{0:T(1024)} %copy-done.9, pred[2048]{0:T(1024)(128)(4,1)} %copy-done.11, bf16[2048,4,128]{2,0,1:T(8,128)(2,1)} %bitcast.142, ...), kind=kLoop, calls=%fused_computation.82 | loop fusion | flops 4718080 | bytes 3166208 | tf_op jit(solution)/shard_map/reduce_sum | solution.py:27
  188.5 2.5 fusion.43
  191.1 2.1 fusion.42
  193.5 1.5 copy.45
  195.0 5.2 %all-to-all-start.1 = ((bf16[32,64,4,128]{3,1,2,0:T(8,128)(2,1)}), bf16[32,64,4,128]{3,1,2,0:T(8,128)(2,1)S(1)}, u32[]{:S(2)}, u32[]{:S(2)}) async-start(bf16[32,64,4,128]{3,1,2,0:T(8,128)(2,1)} %copy.45), calls=%async_computation.1 | async-start | bytes 4194304 | tf_op jit(solution)/shard_map/all_to_all | solution.py:120
  200.2 164.9 %psum.7 = f32[4,128]{1,0:T(4,128)} all-reduce(f32[4,128]{1,0:T(4,128)S(1)} %pad_maximum_fusion.2), channel_id=1, replica_groups=mesh['dp'=4,'seq'=32,'head'=4] {'dp','seq','head'}, use_global_device_ids=true, to_apply=%region_13.14 | all-reduce | flops 512 | bytes 4096 | tf_op jit(solution)/shard_map/psum | solution.py:130
  365.5 0.6 slice_bitcast_fusion.1
  366.1 0.7 slice.89
  366.8 0.8 slice_bitcast_fusion
  367.6 1.2 slice.90
  (124 shorter events, 3.7 us)
Async XLA Ops:
  3.2 18.5 %copy-start.22 = (s32[8]{0:T(128)S(1)}, s32[8]{0:T(128)}, u32[]{:S(2)}) copy-start(s32[8]{0:T(128)} %param.12) | copy-start | bytes 100
  3.2 19.1 %copy-start.21 = (f32[4,128]{1,0:T(4,128)S(1)}, f32[4,128]{1,0:T(4,128)}, u32[]{:S(2)}) copy-start(f32[4,128]{1,0:T(4,128)} %param.13) | copy-start | bytes 6148
  4.7 115.4 %all-to-all-start = ((bf16[32,64,4,128]{3,1,2,0:T(8,128)(2,1)}), bf16[32,64,4,128]{3,1,2,0:T(8,128)(2,1)}, u32[]{:S(2)}, u32[]{:S(2)}) async-start(bf16[32,64,4,128]{3,1,2,0:T(8,128)(2,1)} %copy.38), calls=%async_computation | async-start | bytes 4194304 | tf_op jit(solution)/shard_map/all_to_all | solution.py:47
  22.3 103.0 %copy-start.11 = (pred[2048]{0:T(1024)(128)(4,1)}, pred[2048]{0:T(1024)(128)(4,1)S(1)}, u32[]{:S(2)}) copy-start(pred[2048]{0:T(1024)(128)(4,1)S(1)} %fusion.51) | copy-start | bytes 6148
  22.3 103.0 %copy-start.13 = (f32[128]{0:T(128)}, f32[128]{0:T(128)S(1)}, u32[]{:S(2)}) copy-start(f32[128]{0:T(128)S(1)} %get-tuple-element.199) | copy-start | bytes 1540
  22.3 103.0 %copy-start.15 = (f32[128]{0:T(128)}, f32[128]{0:T(128)S(1)}, u32[]{:S(2)}) copy-start(f32[128]{0:T(128)S(1)} %get-tuple-element.200) | copy-start | bytes 1540
  22.3 103.0 %copy-start.17 = (f32[128]{0:T(128)}, f32[128]{0:T(128)S(1)}, u32[]{:S(2)}) copy-start(f32[128]{0:T(128)S(1)} %get-tuple-element.201) | copy-start | bytes 1540
  22.3 103.0 %copy-start.19 = (f32[128]{0:T(128)}, f32[128]{0:T(128)S(1)}, u32[]{:S(2)}) copy-start(f32[128]{0:T(128)S(1)} %get-tuple-element.202) | copy-start | bytes 1540
  122.0 1.8 copy-start.2
  123.7 1.7 copy-start.9
  125.4 1.3 copy-start.23
  128.3 1.8 copy-start.6
  129.2 2.6 copy-start
  131.9 4.4 %copy-start.1 = (f32[512,2048]{1,0:T(8,128)S(1)}, f32[512,2048]{1,0:T(8,128)}, u32[]{:S(2)}) copy-start(f32[512,2048]{1,0:T(8,128)} %copy-done) | copy-start | bytes 12582916 | tf_op jit(solution)/shard_map/while
  131.9 4.4 %copy-start.7 = (bf16[2048,1,128]{2,0,1:T(8,128)(2,1)S(1)}, bf16[2048,1,128]{2,0,1:T(8,128)(2,1)}, u32[]{:S(2)}) copy-start(bf16[2048,1,128]{2,0,1:T(8,128)(2,1)} %get-tuple-element.319) | copy-start | bytes 1572868 | tf_op jit(solution)/shard_map/while
  131.9 4.4 %copy-start.25 = (f32[512]{0:T(512)S(1)}, f32[512]{0:T(512)}, u32[]{:S(2)}) copy-start(f32[512]{0:T(512)} %get-tuple-element.278) | copy-start | bytes 6148 | tf_op jit(solution)/shard_map/while
  137.6 1.9 copy-start.24
  139.5 1.3 copy-start.23
  142.5 1.8 copy-start.6
  143.3 2.6 copy-start
  146.1 4.3 %copy-start.1 = (f32[512,2048]{1,0:T(8,128)S(1)}, f32[512,2048]{1,0:T(8,128)}, u32[]{:S(2)}) copy-start(f32[512,2048]{1,0:T(8,128)} %copy-done) | copy-start | bytes 12582916 | tf_op jit(solution)/shard_map/while
  146.1 4.3 %copy-start.7 = (bf16[2048,1,128]{2,0,1:T(8,128)(2,1)S(1)}, bf16[2048,1,128]{2,0,1:T(8,128)(2,1)}, u32[]{:S(2)}) copy-start(bf16[2048,1,128]{2,0,1:T(8,128)(2,1)} %get-tuple-element.319) | copy-start | bytes 1572868 | tf_op jit(solution)/shard_map/while
  146.1 4.3 %copy-start.25 = (f32[512]{0:T(512)S(1)}, f32[512]{0:T(512)}, u32[]{:S(2)}) copy-start(f32[512]{0:T(512)} %get-tuple-element.278) | copy-start | bytes 6148 | tf_op jit(solution)/shard_map/while
  151.7 1.9 copy-start.24
  153.7 1.3 copy-start.23
  156.6 1.8 copy-start.6
  157.5 2.6 copy-start
  160.2 4.4 %copy-start.1 = (f32[512,2048]{1,0:T(8,128)S(1)}, f32[512,2048]{1,0:T(8,128)}, u32[]{:S(2)}) copy-start(f32[512,2048]{1,0:T(8,128)} %copy-done) | copy-start | bytes 12582916 | tf_op jit(solution)/shard_map/while
  160.2 4.4 %copy-start.7 = (bf16[2048,1,128]{2,0,1:T(8,128)(2,1)S(1)}, bf16[2048,1,128]{2,0,1:T(8,128)(2,1)}, u32[]{:S(2)}) copy-start(bf16[2048,1,128]{2,0,1:T(8,128)(2,1)} %get-tuple-element.319) | copy-start | bytes 1572868 | tf_op jit(solution)/shard_map/while
  160.2 4.4 %copy-start.25 = (f32[512]{0:T(512)S(1)}, f32[512]{0:T(512)}, u32[]{:S(2)}) copy-start(f32[512]{0:T(512)} %get-tuple-element.278) | copy-start | bytes 6148 | tf_op jit(solution)/shard_map/while
  165.9 1.9 copy-start.24
  167.9 1.3 copy-start.23
  170.8 1.8 copy-start.6
  171.6 2.6 copy-start
  174.4 4.4 %copy-start.1 = (f32[512,2048]{1,0:T(8,128)S(1)}, f32[512,2048]{1,0:T(8,128)}, u32[]{:S(2)}) copy-start(f32[512,2048]{1,0:T(8,128)} %copy-done) | copy-start | bytes 12582916 | tf_op jit(solution)/shard_map/while
  174.4 4.4 %copy-start.7 = (bf16[2048,1,128]{2,0,1:T(8,128)(2,1)S(1)}, bf16[2048,1,128]{2,0,1:T(8,128)(2,1)}, u32[]{:S(2)}) copy-start(bf16[2048,1,128]{2,0,1:T(8,128)(2,1)} %get-tuple-element.319) | copy-start | bytes 1572868 | tf_op jit(solution)/shard_map/while
  174.4 4.4 %copy-start.25 = (f32[512]{0:T(512)S(1)}, f32[512]{0:T(512)}, u32[]{:S(2)}) copy-start(f32[512]{0:T(512)} %get-tuple-element.278) | copy-start | bytes 6148 | tf_op jit(solution)/shard_map/while
  180.0 1.9 copy-start.24
  182.0 6.5 %copy-start.10 = (f32[2048]{0:T(1024)S(1)}, f32[2048]{0:T(1024)}, u32[]{:S(2)}) copy-start(f32[2048]{0:T(1024)} %copy-done.9) | copy-start | bytes 24580
  182.0 6.5 %copy-start.12 = (pred[2048]{0:T(1024)(128)(4,1)S(1)}, pred[2048]{0:T(1024)(128)(4,1)}, u32[]{:S(2)}) copy-start(pred[2048]{0:T(1024)(128)(4,1)} %copy-done.11) | copy-start | bytes 6148
  182.0 6.5 %copy-start.14 = (f32[128]{0:T(128)S(1)}, f32[128]{0:T(128)}, u32[]{:S(2)}) copy-start(f32[128]{0:T(128)} %copy-done.13) | copy-start | bytes 1540
  182.0 6.5 %copy-start.16 = (f32[128]{0:T(128)S(1)}, f32[128]{0:T(128)}, u32[]{:S(2)}) copy-start(f32[128]{0:T(128)} %copy-done.15) | copy-start | bytes 1540
  182.0 6.5 %copy-start.18 = (f32[128]{0:T(128)S(1)}, f32[128]{0:T(128)}, u32[]{:S(2)}) copy-start(f32[128]{0:T(128)} %copy-done.17) | copy-start | bytes 1540
  182.0 6.5 %copy-start.20 = (f32[128]{0:T(128)S(1)}, f32[128]{0:T(128)}, u32[]{:S(2)}) copy-start(f32[128]{0:T(128)} %copy-done.19) | copy-start | bytes 1540
  183.1 5.5 %copy-start.3 = (bf16[32,64,4,128]{3,1,0,2:T(8,128)(2,1)S(1)}, bf16[32,64,4,128]{3,1,0,2:T(8,128)(2,1)}, u32[]{:S(2)}) copy-start(bf16[32,64,4,128]{3,1,0,2:T(8,128)(2,1)} %copy-done.2) | copy-start | bytes 6291460
  184.4 6.7 %copy-start.4 = (bf16[4,512,1,128]{3,1,2,0:T(8,128)(2,1)S(1)}, bf16[4,512,1,128]{3,1,2,0:T(8,128)(2,1)}, u32[]{:S(2)}) copy-start(bf16[4,512,1,128]{3,1,2,0:T(8,128)(2,1)} %get-tuple-element.65) | copy-start | bytes 1572868
  184.4 8.8 %copy-start.5 = (bf16[2048,1,128]{2,0,1:T(8,128)(2,1)S(1)}, bf16[2048,1,128]{2,0,1:T(8,128)(2,1)}, u32[]{:S(2)}) copy-start(bf16[2048,1,128]{2,0,1:T(8,128)(2,1)} %copy.43) | copy-start | bytes 1572868
  184.4 8.8 %copy-start.8 = (bf16[4,512,1,128]{3,1,0,2:T(8,128)(2,1)S(1)}, bf16[4,512,1,128]{3,1,0,2:T(8,128)(2,1)}, u32[]{:S(2)}) copy-start(bf16[4,512,1,128]{3,1,0,2:T(8,128)(2,1)} %get-tuple-element.68) | copy-start | bytes 1572868
  195.0 170.1 %all-to-all-start.1 = ((bf16[32,64,4,128]{3,1,2,0:T(8,128)(2,1)}), bf16[32,64,4,128]{3,1,2,0:T(8,128)(2,1)S(1)}, u32[]{:S(2)}, u32[]{:S(2)}) async-start(bf16[32,64,4,128]{3,1,2,0:T(8,128)(2,1)} %copy.45), calls=%async_computation.1 | async-start | bytes 4194304 | tf_op jit(solution)/shard_map/all_to_all | solution.py:120
where the time goes:
time: 369 us
  blocking collectives  165 us (45%)
  waiting for transfers between devices  97.8 us (27%)
  matrix products  37.2 us (10%)
  local copies, waits for them, and re-layouts  23.1 us (6%)
  starting transfers between devices  22 us (6%)
  other arithmetic  19.4 us (5%)
    psum x1, blocking collectives, shards(): lax.psum(jnp.stack([q_image, k_image, q_text, k_text]), ('dp', 'seq', 'he...  165 us
    all_to_all x1, waiting for transfers between devices, shards(): lax.all_to_all(outgoing, 'seq', split_axis=0, concat_axis=0, tiled=True)  97.8 us
    all_to_all x1, starting transfers between devices, shards(): lax.all_to_all(outgoing, 'seq', split_axis=0, concat_axis=0, tiled=True)  16.8 us
    dot_general x4, matrix products, one_block(): jnp.einsum('hqk,qhd->khd', weights_low, cot_block, preferred_element_type...  14.6 us
  transfers between devices with their start and end apart: 2, of which 1 were waited for; matrix products, arithmetic and copies ran while one was open for 0% of the time, Pallas kernels for 0%

commit v1 on v0

v1 whole, which is shorter than its diff:
```python
import functools
import math

import jax
import jax.numpy as jnp
from jax import lax
from jax.experimental import pallas as pl
from jax.experimental.pallas import tpu as pltpu
from jax.sharding import PartitionSpec as P

EPSILON = 1e-06
MESH = pl.DeviceIdType.MESH
F32 = jnp.float32
BF16 = jnp.bfloat16
GROUP = 4


def partners(slot, me, count):
    chips = count // 2
    hop = lax.div(slot + 2, 4)
    side = lax.div(lax.rem(slot + 2, 4), 2)
    move = hop * (1 - 2 * side)
    chip, core = lax.div(me, 2), lax.rem(lax.rem(me, 2) + lax.rem(slot, 2), 2)
    to = lax.rem(chip + move + chips, chips) * 2 + core
    source = lax.rem(chip - move + chips, chips) * 2 + core
    return to, source


def nt(a, b):
    return lax.dot_general(a, b, (((1,), (1,)), ((), ())), preferred_element_type=F32)


def nn(a, b):
    return lax.dot_general(a, b, (((1,), (0,)), ((), ())), preferred_element_type=F32)


def attend(
    count,
    samples,
    text_block,
    block,
    dhead,
    others,
    txt_hbm,
    img_hbm,
    txt_cot_hbm,
    img_cot_hbm,
    length_ref,
    gains_ref,
    returned,
    gain_out,
    txt,
    img,
    txt_cot,
    img_cot,
    outgoing,
    arrived,
    results,
    keys,
    keys_turned,
    values_turned,
    bias,
    scores,
    key_total,
    value_total,
    gain_home,
    gain_ring,
    gain_mine,
    gain_plane,
    stage_sem,
    in_send,
    in_recv,
    back_send,
    back_recv,
    ring_send,
    ring_recv,
    plane_send,
    plane_recv,
):
    me = lax.axis_index("seq")
    dp = lax.axis_index("dp")
    head = lax.axis_index("head")
    groups = count // samples
    tile = GROUP * block
    tiles = count // GROUP
    scale = 1.0 / math.sqrt(dhead)
    planes = others[0] * others[1]
    here = dp * others[1] + head

    staged = [
        pltpu.make_async_copy(source, target, stage_sem.at[i])
        for i, (source, target) in enumerate(
            ((img_hbm, img), (txt_hbm, txt), (img_cot_hbm, img_cot), (txt_cot_hbm, txt_cot))
        )
    ]
    for copy in staged:
        copy.start()

    def plane_device(step):
        other = lax.rem(here + step, planes)
        return (lax.div(other, others[1]), me, lax.rem(other, others[1]))

    barrier = pltpu.get_barrier_semaphore()

    def greet(slot, carry):
        to, _ = partners(slot, me, count)
        pl.semaphore_signal(barrier, inc=1, device_id=(dp, to, head), device_id_type=MESH)
        return carry

    def greet_plane(step, carry):
        pl.semaphore_signal(barrier, inc=1, device_id=plane_device(step), device_id_type=MESH)
        return carry

    lax.fori_loop(1, count, greet, 0)
    lax.fori_loop(1, planes, greet_plane, 0)

    def joined(text_part, image_part):
        return jnp.concatenate([text_part.astype(F32), image_part.astype(F32)], axis=0).astype(BF16)

    def pack_pair(first, read_first, read_second):
        def pack(target, carry):
            sample = lax.div(target, groups)
            column = pl.multiple_of(lax.rem(target, groups) * dhead, dhead)
            outgoing[target, first] = read_first(sample, column)
            outgoing[target, first + 1] = read_second(sample, column)
            return carry

        lax.fori_loop(0, count, pack, 0)
        arrived[0, first] = outgoing[me, first]
        arrived[0, first + 1] = outgoing[me, first + 1]

    def raw(which):
        def read(sample, column):
            at = pl.ds(column, dhead)
            return joined(txt[sample, which, :, at], img[sample, which, :, at])

        return read

    def cotangent(sample, column):
        at = pl.ds(column, dhead)
        return joined(txt_cot[sample, :, at], img_cot[sample, :, at])

    def inward(slot, part):
        to, _ = partners(slot, me, count)
        return pltpu.make_async_remote_copy(
            src_ref=outgoing.at[to, pl.ds(2 * part, 2)],
            dst_ref=arrived.at[slot, pl.ds(2 * part, 2)],
            send_sem=in_send.at[part, slot],
            recv_sem=in_recv.at[part, slot],
            device_id=(dp, to, head),
            device_id_type=MESH,
        )

    def outward(slot, part):
        _, source = partners(slot, me, count)
        return pltpu.make_async_remote_copy(
            src_ref=results.at[slot, pl.ds(2 * part, 2)],
            dst_ref=returned.at[me, pl.ds(2 * part, 2)],
            send_sem=back_send.at[part, slot],
            recv_sem=back_recv.at[part, me],
            device_id=(dp, source, head),
            device_id_type=MESH,
        )

    def home(source, part):
        return pltpu.make_async_remote_copy(
            src_ref=results.at[0, pl.ds(2 * part, 2)],
            dst_ref=returned.at[source, pl.ds(2 * part, 2)],
            send_sem=back_send.at[part, 0],
            recv_sem=back_recv.at[part, source],
            device_id=(dp, source, head),
            device_id_type=MESH,
        )

    def each(low, high, body):
        def step(index, carry):
            body(index)
            return carry

        lax.fori_loop(low, high, step, 0)

    staged[0].wait()
    staged[1].wait()
    pack_pair(0, raw(1), raw(2))
    pl.semaphore_wait(barrier, count - 1 + planes - 1)
    each(1, count, lambda slot: inward(slot, 0).start())
    staged[2].wait()
    staged[3].wait()
    pack_pair(2, raw(0), cotangent)
    each(1, count, lambda slot: inward(slot, 1).start())

    place = lax.broadcasted_iota(jnp.int32, (block, dhead), 0)
    is_text = place < text_block

    def gain_rows(text_gain, image_gain):
        one = jnp.where(
            is_text,
            jnp.broadcast_to(gains_ref[pl.ds(text_gain, 1), :], (block, dhead)),
            jnp.broadcast_to(gains_ref[pl.ds(image_gain, 1), :], (block, dhead)),
        )
        return jnp.concatenate([one] * GROUP, axis=0)

    query_gain = gain_rows(2, 0)
    key_gain = gain_rows(3, 1)
    length = length_ref[lax.div(me, groups)]

    def mask(slot):
        _, source = partners(slot, me, count)
        row = lax.broadcasted_iota(jnp.int32, (block, 1), 0)
        dead = jnp.logical_and(row < text_block, row + source * text_block >= length)
        bias[pl.ds(pl.multiple_of(slot * block, block), block), :] = jnp.where(dead, -jnp.inf, 0.0)

    each(0, count, mask)
    key_total[...] = jnp.zeros_like(key_total)
    value_total[...] = jnp.zeros_like(value_total)

    def rows_of(index):
        return pl.ds(pl.multiple_of(index * tile, tile), tile)

    def block_of(ref, index, part):
        return ref[pl.ds(index * GROUP, GROUP), part].reshape(tile, dhead)

    def normed(raw_rows):
        inverse = lax.rsqrt(jnp.mean(raw_rows * raw_rows, axis=-1, keepdims=True) + EPSILON)
        return raw_rows * inverse, inverse

    def split_sums(terms):
        parts = terms.reshape(GROUP, block, dhead)
        text_sum = jnp.sum(parts[:, :text_block].reshape(-1, dhead), axis=0, keepdims=True)
        image_sum = jnp.sum(parts[:, text_block:].reshape(-1, dhead), axis=0, keepdims=True)
        return text_sum, image_sum

    def raw_gradient(scaled_grad, rows, inverse, gain):
        grad_rows = scaled_grad * gain
        inner = jnp.mean(grad_rows * rows, axis=-1, keepdims=True)
        return (inverse * (grad_rows - rows * inner)).astype(BF16)

    def prepare(index):
        each(
            jnp.maximum(index * GROUP, 1),
            (index + 1) * GROUP,
            lambda slot: inward(slot, 0).wait_recv(),
        )
        rows, _ = normed(block_of(arrived, index, 0).astype(F32))
        scaled = rows * key_gain
        keys[rows_of(index), :] = scaled.astype(BF16)
        keys_turned[:, rows_of(index)] = scaled.T.astype(BF16)
        values_turned[:, rows_of(index)] = block_of(arrived, index, 1).astype(F32).T.astype(BF16)

    each(0, tiles, prepare)

    def one_tile(index, carry):
        text_gain, image_gain = carry
        each(
            jnp.maximum(index * GROUP, 1),
            (index + 1) * GROUP,
            lambda slot: inward(slot, 1).wait_recv(),
        )
        rows, inverse = normed(block_of(arrived, index, 2).astype(F32))
        query = (rows * query_gain).astype(BF16)
        cot = block_of(arrived, index, 3)

        def score(part, peak):
            at = rows_of(part)
            here_scores = nt(keys[at, :], query) * scale + bias[at, :]
            scores[at, :] = here_scores
            return jnp.maximum(peak, jnp.max(here_scores, axis=0, keepdims=True))

        peak = lax.fori_loop(0, tiles, score, jnp.full((1, tile), -jnp.inf, F32))

        def exponent(part, total):
            at = rows_of(part)
            power = jnp.exp(scores[at, :] - peak)
            scores[at, :] = power
            return total + jnp.sum(power, axis=0, keepdims=True)

        total = lax.fori_loop(0, tiles, exponent, jnp.zeros((1, tile), F32))
        share = 1.0 / total

        def weigh(part, attended):
            at = rows_of(part)
            weights = scores[at, :] * share
            scores[at, :] = weights
            low = weights.astype(BF16)
            value_total[at, :] += nn(low, cot)
            return attended + nn(values_turned[:, at], low)

        attended = lax.fori_loop(0, tiles, weigh, jnp.zeros((dhead, tile), F32))
        attended = attended.astype(BF16).astype(F32)
        delta = jnp.sum(attended * cot.astype(F32).T, axis=0, keepdims=True)

        def differentiate(part, grad_query):
            at = rows_of(part)
            grad_weights = nt(block_of(arrived, part, 1), cot)
            grad_scores = (scores[at, :] * (grad_weights - delta)).astype(BF16)
            key_total[at, :] += nn(grad_scores, query)
            return grad_query + nn(keys_turned[:, at], grad_scores)

        grad_query = lax.fori_loop(0, tiles, differentiate, jnp.zeros((dhead, tile), F32))
        grad_query = (grad_query * scale).astype(BF16).astype(F32).T
        text_sum, image_sum = split_sums(grad_query * rows)
        slots = pl.ds(index * GROUP, GROUP)
        results[slots, 0] = raw_gradient(grad_query, rows, inverse, query_gain).reshape(
            GROUP, block, dhead
        )
        results[slots, 1] = attended.T.astype(BF16).reshape(GROUP, block, dhead)
        each(
            jnp.maximum(index * GROUP, 1),
            (index + 1) * GROUP,
            lambda slot: outward(slot, 0).start(),
        )
        return (text_gain + text_sum, image_gain + image_sum)

    nothing = jnp.zeros((1, dhead), F32)
    query_text, query_image = lax.fori_loop(0, tiles, one_tile, (nothing, nothing))

    def finish(index, carry):
        text_gain, image_gain = carry
        at = rows_of(index)
        rows, inverse = normed(block_of(arrived, index, 0).astype(F32))
        grad_key = (key_total[at, :] * scale).astype(BF16).astype(F32)
        text_sum, image_sum = split_sums(grad_key * rows)
        slots = pl.ds(index * GROUP, GROUP)
        results[slots, 2] = raw_gradient(grad_key, rows, inverse, key_gain).reshape(
            GROUP, block, dhead
        )
        results[slots, 3] = value_total[at, :].astype(BF16).reshape(GROUP, block, dhead)
        return (text_gain + text_sum, image_gain + image_sum)

    key_text, key_image = lax.fori_loop(0, tiles, finish, (nothing, nothing))

    gain_home[...] = jnp.concatenate([query_image, key_image, query_text, key_text], axis=0)

    def ring_copy(slot):
        to, _ = partners(slot, me, count)
        return pltpu.make_async_remote_copy(
            src_ref=gain_home,
            dst_ref=gain_ring.at[me],
            send_sem=ring_send.at[slot],
            recv_sem=ring_recv.at[me],
            device_id=(dp, to, head),
            device_id_type=MESH,
        )

    def ring_arrival(slot):
        _, source = partners(slot, me, count)
        return pltpu.make_async_remote_copy(
            src_ref=gain_home,
            dst_ref=gain_ring.at[source],
            send_sem=ring_send.at[slot],
            recv_sem=ring_recv.at[source],
            device_id=(dp, source, head),
            device_id_type=MESH,
        )

    def plane_copy(step):
        return pltpu.make_async_remote_copy(
            src_ref=gain_mine,
            dst_ref=gain_plane.at[here],
            send_sem=plane_send.at[step],
            recv_sem=plane_recv.at[here],
            device_id=plane_device(step),
            device_id_type=MESH,
        )

    def plane_arrival(step):
        other = lax.rem(here + step, planes)
        return pltpu.make_async_remote_copy(
            src_ref=gain_mine,
            dst_ref=gain_plane.at[other],
            send_sem=plane_send.at[step],
            recv_sem=plane_recv.at[other],
            device_id=plane_device(step),
            device_id_type=MESH,
        )

    each(1, count, lambda slot: ring_copy(slot).start())
    each(1, count, lambda slot: outward(slot, 1).start())
    returned[me] = results[0]
    gain_ring[me] = gain_home[...]
    each(1, count, lambda slot: ring_arrival(slot).wait_recv())
    gain_mine[...] = jnp.sum(gain_ring[...], axis=0)
    each(1, planes, lambda step: plane_copy(step).start())
    gain_plane[here] = gain_mine[...]
    each(1, planes, lambda step: plane_arrival(step).wait_recv())
    gain_out[...] = jnp.sum(gain_plane[...], axis=0)

    def drain(slot):
        inward(slot, 0).wait_send()
        inward(slot, 1).wait_send()
        ring_copy(slot).wait_send()
        outward(slot, 0).wait_send()
        outward(slot, 1).wait_send()

    each(1, count, drain)
    each(1, planes, lambda step: plane_copy(step).wait_send())

    def collect(slot):
        to, _ = partners(slot, me, count)
        home(to, 0).wait_recv()
        home(to, 1).wait_recv()

    each(1, count, collect)


def unpack(groups, text_block, dhead, returned, txt_out, img_out, txt_grads, img_grads):
    for group in range(groups):
        at = pl.ds(group * dhead, dhead)
        for sample in range(txt_out.shape[0]):
            for part in range(4):
                rows = returned[sample * groups + group, part].astype(F32)
                text_rows = rows[:text_block].astype(BF16)
                image_rows = rows[text_block:].astype(BF16)
                if part == 1:
                    txt_out[sample, :, at] = text_rows
                    img_out[sample, :, at] = image_rows
                else:
                    place = max(part - 1, 0)
                    txt_grads[sample, place, :, at] = text_rows
                    img_grads[sample, place, :, at] = image_rows


def shards(others, txt_qkv, img_qkv, txt_grad_out, img_grad_out, caption_len, norm_gains):
    count = lax.axis_size("seq")
    samples, text_block = txt_qkv.shape[:2]
    image_block, width = img_qkv.shape[1], img_qkv.shape[3]
    dhead = norm_gains.shape[1]
    block = text_block + image_block
    groups = count // samples
    rows = count * block
    tile = GROUP * block
    planes = others[0] * others[1]
    txt = txt_qkv.transpose(0, 2, 1, 3)
    img = img_qkv.transpose(0, 2, 1, 3)
    wire = (count, 4, block, dhead)
    in_vmem = pl.BlockSpec(memory_space=pltpu.VMEM)
    anywhere = pl.BlockSpec(memory_space=pl.ANY)
    dma = pltpu.SemaphoreType.DMA
    returned, gain_grad = pl.pallas_call(
        functools.partial(attend, count, samples, text_block, block, dhead, others),
        out_shape=(
            jax.ShapeDtypeStruct(wire, BF16),
            jax.ShapeDtypeStruct((4, dhead), F32),
        ),
        in_specs=[anywhere] * 4 + [pl.BlockSpec(memory_space=pltpu.SMEM), in_vmem],
        out_specs=(in_vmem, in_vmem),
        scratch_shapes=[
            pltpu.VMEM(txt.shape, BF16),
            pltpu.VMEM(img.shape, BF16),
            pltpu.VMEM(txt_grad_out.shape, BF16),
            pltpu.VMEM(img_grad_out.shape, BF16),
            pltpu.VMEM(wire, BF16),
            pltpu.VMEM(wire, BF16),
            pltpu.VMEM(wire, BF16),
            pltpu.VMEM((rows, dhead), BF16),
            pltpu.VMEM((dhead, rows), BF16),
            pltpu.VMEM((dhead, rows), BF16),
            pltpu.VMEM((rows, 1), F32),
            pltpu.VMEM((rows, tile), F32),
            pltpu.VMEM((rows, dhead), F32),
            pltpu.VMEM((rows, dhead), F32),
            pltpu.VMEM((4, dhead), F32),
            pltpu.VMEM((count, 4, dhead), F32),
            pltpu.VMEM((4, dhead), F32),
            pltpu.VMEM((planes, 4, dhead), F32),
            dma((4,)),
            dma((2, count)),
            dma((2, count)),
            dma((2, count)),
            dma((2, count)),
            dma((count,)),
            dma((count,)),
            dma((planes,)),
            dma((planes,)),
        ],
        compiler_params=pltpu.CompilerParams(
            collective_id=0, has_side_effects=True, vmem_limit_bytes=44 * 2**20
        ),
        name="attend",
    )(txt, img, txt_grad_out, img_grad_out, caption_len, norm_gains)
    part = 4
    txt_out, img_out, txt_grads, img_grads = pl.pallas_call(
        functools.partial(unpack, groups, text_block, dhead),
        grid=(samples // part,),
        out_shape=(
            jax.ShapeDtypeStruct((samples, text_block, width), BF16),
            jax.ShapeDtypeStruct((samples, image_block, width), BF16),
            jax.ShapeDtypeStruct((samples, 3, text_block, width), BF16),
            jax.ShapeDtypeStruct((samples, 3, image_block, width), BF16),
        ),
        in_specs=[pl.BlockSpec((part * groups, 4, block, dhead), lambda i: (i, 0, 0, 0))],
        out_specs=(
            pl.BlockSpec((part, text_block, width), lambda i: (i, 0, 0)),
            pl.BlockSpec((part, image_block, width), lambda i: (i, 0, 0)),
            pl.BlockSpec((part, 3, text_block, width), lambda i: (i, 0, 0, 0)),
            pl.BlockSpec((part, 3, image_block, width), lambda i: (i, 0, 0, 0)),
        ),
        compiler_params=pltpu.CompilerParams(vmem_limit_bytes=32 * 2**20),
        name="unpack",
    )(returned)
    return (
        txt_out,
        img_out,
        txt_grads.transpose(0, 2, 1, 3),
        img_grads.transpose(0, 2, 1, 3),
        gain_grad,
    )


def solution(mesh):
    others = (mesh.shape["dp"], mesh.shape["head"])
    placed = (
        P("dp", "seq", None, "head"),
        P("dp", "seq", None, "head"),
        P("dp", "seq", "head"),
        P("dp", "seq", "head"),
        P("dp"),
        P(),
    )
    return jax.shard_map(
        functools.partial(shards, others),
        mesh=mesh,
        in_specs=placed,
        out_specs=(
            P("dp", "seq", "head"),
            P("dp", "seq", "head"),
            P("dp", "seq", None, "head"),
            P("dp", "seq", None, "head"),
            P(),
        ),
        check_vma=False,
    )
```

time: 369 us -> 217 us (0.59)
  Pallas kernels: 0 us -> 210 us
  blocking collectives: 165 us -> 0 us
  waiting for transfers between devices: 97.8 us -> 0 us
  matrix products: 37.2 us -> 0 us
  starting transfers between devices: 22 us -> 0 us
  other arithmetic: 19.4 us -> 0 us
  local copies, waits for them, and re-layouts: 23.1 us -> 6.03 us
    pallas_call x0 -> x2, Pallas kernels: none -> 210 us  [the longest x1 209 us: shards(): pl.pallas_call(functools.partial(attend, count, samples, text_block, bloc...]
    psum x1 -> x0, blocking collectives: 165 us -> none  [shards(): lax.psum(jnp.stack([q_image, k_image, q_text, k_text]), ('dp', 'seq', 'he...]
    all_to_all x2 -> x0, waiting for transfers between devices: 97.8 us -> none  [the longest x1 97.8 us: shards(): lax.all_to_all(outgoing, 'seq', split_axis=0, concat_axis=0, tiled=True)]
    dot_general x24 -> x0, matrix products: 37.2 us -> none  [the longest x4 14.6 us: one_block(): jnp.einsum('hqk,qhd->khd', weights_low, cot_block, preferred_element_type...]
    all_to_all x2 -> x0, starting transfers between devices: 22 us -> none  [the longest x1 16.8 us: shards(): lax.all_to_all(outgoing, 'seq', split_axis=0, concat_axis=0, tiled=True)]
    reduce_sum x7 -> x0, other arithmetic: 11 us -> none  [the longest x1 4.09 us: rms_backward(): image_part = jnp.sum(jnp.where(text_rows[:, None], 0.0, per_row), axis=0)]
    dynamic_slice x13 -> x0, local copies, waits for them, and re-layouts: 7.13 us -> none  [the longest x8 4.14 us: one_block(): cot_block = lax.dynamic_slice_in_dim(cot_heads, start, tile, 0)]
    unnamed x38 -> x13, local copies, waits for them, and re-layouts: 0.09 us -> 6.03 us
  transfers between devices with their start and end apart: 2 -> 0, of which waited for: 1 -> 0; matrix products, arithmetic and copies ran while one was open for 0% -> 0% of each run, Pallas kernels for 0% -> 0%
where the time goes in v1:
time: 217 us
  Pallas kernels  210 us (97%)
  local copies, waits for them, and re-layouts  6.03 us (3%)
    pallas_call x1, Pallas kernels, shards(): pl.pallas_call(functools.partial(attend, count, samples, text_block, bloc...  209 us
    unnamed x13, local copies, waits for them, and re-layouts  6.03 us

profile of v1, /device:TPU:1, one launch (start us, length us, event | category | flops | bytes accessed | tf_op | source)
XLA Modules:
  0.0 216.9 jit_solution(3884575254355583233)
XLA Ops:
  0.6 0.0 copy-start
  0.6 1.3 copy-done
  2.0 0.0 copy-start.1
  2.0 1.0 copy-done.1
  3.0 0.0 copy-start.2
  3.0 0.9 copy-done.2
  3.9 0.0 copy-start.3
  3.9 0.8 copy-done.3
  4.8 0.0 copy-start.4
  4.8 0.7 copy-done.4
  5.4 0.0 copy-start.5
  5.4 0.7 copy-done.5
  6.1 208.7 %attend.1 = (bf16[32,4,64,128]{3,2,1,0:T(8,128)(2,1)S(1)}, f32[4,128]{1,0:T(4,128)S(1)}) custom-call(bf16[8,3,8,512]{3,2,1,0:T(8,128)(2,1)S(1)} %bitcast.5, bf16[8,3,56,512]{3,2,1,0:T(8,128)(2,1)S(1)} %bitcast.4, bf16[8,8,512]{2,1,0:T(8,128)(2,1)S(1)} %copy-done.3, bf16[8,56,512]{2,1,0:T(8,128)(2,1)S(1)} %copy-done.1, s32[8]{0:T(128)S(1)} %copy-done.5, ...), custom_call_target="tpu_custom_call" | custom-call | tf_op jit(solution)/shard_map/attend/pallas_call | solution.py:439
  214.8 1.5 unpack.1
  216.3 0.6 copy.12
Async XLA Ops:
  0.6 1.3 copy-start
  2.0 1.0 copy-start.1
  3.0 0.9 copy-start.2
  3.9 0.8 copy-start.3
  4.8 0.7 copy-start.4
  5.4 0.7 copy-start.5

commit v2 on v1

--- a/solution.py
+++ b/solution.py
@@ -12,11 +12,13 @@
 MESH = pl.DeviceIdType.MESH
 F32 = jnp.float32
 BF16 = jnp.bfloat16
+CUT0, CUT1 = 16, 25
 GROUP = 4
 
 
 def partners(slot, me, count):
     chips = count // 2
+    slot = jnp.where(slot == 0, 0, count - slot)
     hop = lax.div(slot + 2, 4)
     side = lax.div(lax.rem(slot + 2, 4), 2)
     move = hop * (1 - 2 * side)
@@ -45,14 +47,16 @@
     img_hbm,
     txt_cot_hbm,
     img_cot_hbm,
-    length_ref,
-    gains_ref,
+    length_hbm,
+    gains_hbm,
     returned,
     gain_out,
     txt,
     img,
     txt_cot,
     img_cot,
+    length_ref,
+    gains_ref,
     outgoing,
     arrived,
     results,
@@ -66,6 +70,7 @@
     gain_home,
     gain_ring,
     gain_mine,
+    gain_pair,
     gain_plane,
     stage_sem,
     in_send,
@@ -90,7 +95,14 @@
     staged = [
         pltpu.make_async_copy(source, target, stage_sem.at[i])
         for i, (source, target) in enumerate(
-            ((img_hbm, img), (txt_hbm, txt), (img_cot_hbm, img_cot), (txt_cot_hbm, txt_cot))
+            (
+                (img_hbm, img),
+                (txt_hbm, txt),
+                (img_cot_hbm, img_cot),
+                (txt_cot_hbm, txt_cot),
+                (length_hbm, length_ref),
+                (gains_hbm, gains_ref),
+            )
         )
     ]
     for copy in staged:
@@ -117,15 +129,14 @@
     def joined(text_part, image_part):
         return jnp.concatenate([text_part.astype(F32), image_part.astype(F32)], axis=0).astype(BF16)
 
-    def pack_pair(first, read_first, read_second):
-        def pack(target, carry):
-            sample = lax.div(target, groups)
-            column = pl.multiple_of(lax.rem(target, groups) * dhead, dhead)
-            outgoing[target, first] = read_first(sample, column)
-            outgoing[target, first + 1] = read_second(sample, column)
-            return carry
-
-        lax.fori_loop(0, count, pack, 0)
+    def pack(target, first, read_first, read_second):
+        sample = lax.div(target, groups)
+        column = pl.multiple_of(lax.rem(target, groups) * dhead, dhead)
+        outgoing[target, first] = read_first(sample, column)
+        outgoing[target, first + 1] = read_second(sample, column)
+
+    def pack_own(first, read_first, read_second):
+        pack(me, first, read_first, read_second)
         arrived[0, first] = outgoing[me, first]
         arrived[0, first + 1] = outgoing[me, first + 1]
 
@@ -179,16 +190,28 @@
 
         lax.fori_loop(low, high, step, 0)
 
+    def send_keys(slot):
+        to, _ = partners(slot, me, count)
+        pack(to, 0, raw(1), raw(2))
+        inward(slot, 0).start()
+
+    def send_queries(slot):
+        to, _ = partners(slot, me, count)
+        pack(to, 2, raw(0), cotangent)
+        inward(slot, 1).start()
+
     staged[0].wait()
     staged[1].wait()
-    pack_pair(0, raw(1), raw(2))
+    pack_own(0, raw(1), raw(2))
     pl.semaphore_wait(barrier, count - 1 + planes - 1)
-    each(1, count, lambda slot: inward(slot, 0).start())
+    each(1, count, send_keys)
     staged[2].wait()
     staged[3].wait()
-    pack_pair(2, raw(0), cotangent)
-    each(1, count, lambda slot: inward(slot, 1).start())
-
+    each(1, count, send_queries)
+    pack_own(2, raw(0), cotangent)
+
+    staged[4].wait()
+    staged[5].wait()
     place = lax.broadcasted_iota(jnp.int32, (block, dhead), 0)
     is_text = place < text_block
 
@@ -331,69 +354,95 @@
 
     gain_home[...] = jnp.concatenate([query_image, key_image, query_text, key_text], axis=0)
 
+    chip, core = lax.div(me, 2), lax.rem(me, 2)
+    speaks = here == chip
+
     def ring_copy(slot):
         to, _ = partners(slot, me, count)
         return pltpu.make_async_remote_copy(
-            src_ref=gain_home,
-            dst_ref=gain_ring.at[me],
+            src_ref=gain_mine,
+            dst_ref=gain_ring.at[core],
             send_sem=ring_send.at[slot],
-            recv_sem=ring_recv.at[me],
+            recv_sem=ring_recv.at[core],
             device_id=(dp, to, head),
             device_id_type=MESH,
         )
 
-    def ring_arrival(slot):
-        _, source = partners(slot, me, count)
-        return pltpu.make_async_remote_copy(
-            src_ref=gain_home,
-            dst_ref=gain_ring.at[source],
-            send_sem=ring_send.at[slot],
-            recv_sem=ring_recv.at[source],
-            device_id=(dp, source, head),
-            device_id_type=MESH,
-        )
-
-    def plane_copy(step):
+    def ring_arrival(which):
         return pltpu.make_async_remote_copy(
             src_ref=gain_mine,
-            dst_ref=gain_plane.at[here],
-            send_sem=plane_send.at[step],
-            recv_sem=plane_recv.at[here],
+            dst_ref=gain_ring.at[which],
+            send_sem=ring_send.at[0],
+            recv_sem=ring_recv.at[which],
+            device_id=(dp, 2 * here + which, head),
+            device_id_type=MESH,
+        )
+
+    def plane_copy(turn, step):
+        return pltpu.make_async_remote_copy(
+            src_ref=gain_home if turn == 0 else gain_pair,
+            dst_ref=gain_plane.at[turn, here],
+            send_sem=plane_send.at[turn, step],
+            recv_sem=plane_recv.at[turn, here],
             device_id=plane_device(step),
             device_id_type=MESH,
         )
 
-    def plane_arrival(step):
+    def plane_arrival(turn, step):
         other = lax.rem(here + step, planes)
         return pltpu.make_async_remote_copy(
-            src_ref=gain_mine,
-            dst_ref=gain_plane.at[other],
-            send_sem=plane_send.at[step],
-            recv_sem=plane_recv.at[other],
+            src_ref=gain_home if turn == 0 else gain_pair,
+            dst_ref=gain_plane.at[turn, other],
+            send_sem=plane_send.at[turn, step],
+            recv_sem=plane_recv.at[turn, other],
             device_id=plane_device(step),
             device_id_type=MESH,
         )
 
-    each(1, count, lambda slot: ring_copy(slot).start())
-    each(1, count, lambda slot: outward(slot, 1).start())
-    returned[me] = results[0]
-    gain_ring[me] = gain_home[...]
-    each(1, count, lambda slot: ring_arrival(slot).wait_recv())
-    gain_mine[...] = jnp.sum(gain_ring[...], axis=0)
-    each(1, planes, lambda step: plane_copy(step).start())
-    gain_plane[here] = gain_mine[...]
-    each(1, planes, lambda step: plane_arrival(step).wait_recv())
-    gain_out[...] = jnp.sum(gain_plane[...], axis=0)
+    def send_back(low, high):
+        each(low, high, lambda index: outward(index, 1).start())
+
+    each(1, planes, lambda step: plane_copy(0, step).start())
+    gain_plane[0, here] = gain_home[...]
+    mine = pltpu.make_async_copy(results.at[0], returned.at[me], stage_sem.at[0])
+    mine.start()
+    send_back(1, CUT0)
+    each(1, planes, lambda step: plane_arrival(0, step).wait_recv())
+    gain_mine[...] = jnp.sum(gain_plane[0], axis=0)
+
+    @pl.when(speaks)
+    def _():
+        each(1, count, lambda slot: ring_copy(slot).start())
+        gain_ring[core] = gain_mine[...]
+
+    send_back(CUT0, CUT1)
+    for which in range(2):
+
+        @pl.when(2 * here + which != me)
+        def _():
+            ring_arrival(which).wait_recv()
+
+    gain_pair[...] = gain_ring[0] + gain_ring[1]
+    each(1, planes, lambda step: plane_copy(1, step).start())
+    gain_plane[1, here] = gain_pair[...]
+    send_back(CUT1, count)
+    each(1, planes, lambda step: plane_arrival(1, step).wait_recv())
+    gain_out[...] = jnp.sum(gain_plane[1], axis=0)
 
     def drain(slot):
         inward(slot, 0).wait_send()
         inward(slot, 1).wait_send()
-        ring_copy(slot).wait_send()
         outward(slot, 0).wait_send()
         outward(slot, 1).wait_send()
 
     each(1, count, drain)
-    each(1, planes, lambda step: plane_copy(step).wait_send())
+    each(1, planes, lambda step: plane_copy(0, step).wait_send())
+    each(1, planes, lambda step: plane_copy(1, step).wait_send())
+
+    @pl.when(speaks)
+    def _():
+        each(1, count, lambda slot: ring_copy(slot).wait_send())
+
 
     def collect(slot):
         to, _ = partners(slot, me, count)
@@ -401,9 +450,11 @@
         home(to, 1).wait_recv()
 
     each(1, count, collect)
-
-
-def unpack(groups, text_block, dhead, returned, txt_out, img_out, txt_grads, img_grads):
+    mine.wait()
+
+
+def unpack(groups, text_block, dhead, returned, gain_sum, txt_out, img_out, txt_grads, img_grads, gain_grad):
+    gain_grad[...] = gain_sum[...]
     for group in range(groups):
         at = pl.ds(group * dhead, dhead)
         for sample in range(txt_out.shape[0]):
@@ -434,21 +485,23 @@
     img = img_qkv.transpose(0, 2, 1, 3)
     wire = (count, 4, block, dhead)
     in_vmem = pl.BlockSpec(memory_space=pltpu.VMEM)
-    anywhere = pl.BlockSpec(memory_space=pl.ANY)
+    in_hbm = pl.BlockSpec(memory_space=pltpu.HBM)
     dma = pltpu.SemaphoreType.DMA
-    returned, gain_grad = pl.pallas_call(
+    returned, gain_sum = pl.pallas_call(
         functools.partial(attend, count, samples, text_block, block, dhead, others),
         out_shape=(
             jax.ShapeDtypeStruct(wire, BF16),
             jax.ShapeDtypeStruct((4, dhead), F32),
         ),
-        in_specs=[anywhere] * 4 + [pl.BlockSpec(memory_space=pltpu.SMEM), in_vmem],
-        out_specs=(in_vmem, in_vmem),
+        in_specs=[in_hbm] * 6,
+        out_specs=(in_hbm, in_vmem),
         scratch_shapes=[
             pltpu.VMEM(txt.shape, BF16),
             pltpu.VMEM(img.shape, BF16),
             pltpu.VMEM(txt_grad_out.shape, BF16),
             pltpu.VMEM(img_grad_out.shape, BF16),
+            pltpu.SMEM((samples,), jnp.int32),
+            pltpu.VMEM((4, dhead), F32),
             pltpu.VMEM(wire, BF16),
             pltpu.VMEM(wire, BF16),
             pltpu.VMEM(wire, BF16),
@@ -460,26 +513,27 @@
             pltpu.VMEM((rows, dhead), F32),
             pltpu.VMEM((rows, dhead), F32),
             pltpu.VMEM((4, dhead), F32),
-            pltpu.VMEM((count, 4, dhead), F32),
+            pltpu.VMEM((2, 4, dhead), F32),
             pltpu.VMEM((4, dhead), F32),
-            pltpu.VMEM((planes, 4, dhead), F32),
-            dma((4,)),
+            pltpu.VMEM((4, dhead), F32),
+            pltpu.VMEM((2, planes, 4, dhead), F32),
+            dma((6,)),
             dma((2, count)),
             dma((2, count)),
             dma((2, count)),
             dma((2, count)),
             dma((count,)),
-            dma((count,)),
-            dma((planes,)),
-            dma((planes,)),
+            dma((2,)),
+            dma((2, planes)),
+            dma((2, planes)),
         ],
         compiler_params=pltpu.CompilerParams(
-            collective_id=0, has_side_effects=True, vmem_limit_bytes=44 * 2**20
+            collective_id=0, has_side_effects=True, vmem_limit_bytes=60 * 2**20
         ),
         name="attend",
     )(txt, img, txt_grad_out, img_grad_out, caption_len, norm_gains)
     part = 4
-    txt_out, img_out, txt_grads, img_grads = pl.pallas_call(
+    txt_out, img_out, txt_grads, img_grads, gain_grad = pl.pallas_call(
         functools.partial(unpack, groups, text_block, dhead),
         grid=(samples // part,),
         out_shape=(
@@ -487,17 +541,22 @@
             jax.ShapeDtypeStruct((samples, image_block, width), BF16),
             jax.ShapeDtypeStruct((samples, 3, text_block, width), BF16),
             jax.ShapeDtypeStruct((samples, 3, image_block, width), BF16),
+            jax.ShapeDtypeStruct((4, dhead), F32),
         ),
-        in_specs=[pl.BlockSpec((part * groups, 4, block, dhead), lambda i: (i, 0, 0, 0))],
+        in_specs=[
+            pl.BlockSpec((part * groups, 4, block, dhead), lambda i: (i, 0, 0, 0)),
+            pl.BlockSpec((4, dhead), lambda i: (0, 0)),
+        ],
         out_specs=(
             pl.BlockSpec((part, text_block, width), lambda i: (i, 0, 0)),
             pl.BlockSpec((part, image_block, width), lambda i: (i, 0, 0)),
             pl.BlockSpec((part, 3, text_block, width), lambda i: (i, 0, 0, 0)),
             pl.BlockSpec((part, 3, image_block, width), lambda i: (i, 0, 0, 0)),
+            pl.BlockSpec((4, dhead), lambda i: (0, 0)),
         ),
-        compiler_params=pltpu.CompilerParams(vmem_limit_bytes=32 * 2**20),
+        compiler_params=pltpu.CompilerParams(vmem_limit_bytes=60 * 2**20),
         name="unpack",
-    )(returned)
+    )(returned, gain_sum)
     return (
         txt_out,
         img_out,

time: 217 us -> 206 us (0.949)
  local copies, waits for them, and re-layouts: 6.03 us -> 0 us
  Pallas kernels: 210 us -> 205 us
    pallas_call x1, Pallas kernels: 209 us -> 202 us  [shards(): pl.pallas_call(functools.partial(attend, count, samples, text_block, bloc...]
    unnamed x13 -> x0, local copies, waits for them, and re-layouts: 6.03 us -> none
where the time goes in v2:
time: 206 us; the launch traced here: 205 us
  Pallas kernels  205 us (100%)
    pallas_call x1, Pallas kernels, shards(): pl.pallas_call(functools.partial(attend, count, samples, text_block, bloc...  202 us

profile of v2, /device:TPU:1, one launch (start us, length us, event | category | flops | bytes accessed | tf_op | source)
XLA Modules:
  0.0 205.4 jit_solution(17913760882051256029)
XLA Ops:
  0.6 202.0 %attend.1 = (bf16[32,4,64,128]{3,2,1,0:T(8,128)(2,1)}, f32[4,128]{1,0:T(4,128)}) custom-call(bf16[8,3,8,512]{3,2,1,0:T(8,128)(2,1)} %bitcast.5, bf16[8,3,56,512]{3,2,1,0:T(8,128)(2,1)} %bitcast.4, bf16[8,8,512]{2,1,0:T(8,128)(2,1)} %txt_cot_hbm.1, bf16[8,56,512]{2,1,0:T(8,128)(2,1)} %img_cot_hbm.1, s32[8]{0:T(128)} %length_hbm.1, f32[4,128]{1,0:T(4,128)} %gains_hbm.1), custom_call_target="tpu_custom_call" | custom-call | tf_op jit(solution)/shard_map/attend/pallas_call | solution.py:490
  202.7 2.7 %unpack.1 = (bf16[8,8,512]{2,1,0:T(8,128)(2,1)}, bf16[8,56,512]{2,1,0:T(8,128)(2,1)}, bf16[8,3,8,512]{3,2,1,0:T(8,128)(2,1)}, bf16[8,3,56,512]{3,2,1,0:T(8,128)(2,1)}, f32[4,128]{1,0:T(4,128)}) custom-call(bf16[32,4,64,128]{3,2,1,0:T(8,128)(2,1)} %get-tuple-element.12.returned, f32[4,128]{1,0:T(4,128)} %get-tuple-element.13.gain_sum), custom_call_target="tpu_custom_call" | custom-call | tf_op jit(solution)/shard_map/unpack/pallas_call | solution.py:536

commit v3 on v2

--- a/solution.py
+++ b/solution.py
@@ -426,31 +426,31 @@
     each(1, planes, lambda step: plane_copy(1, step).start())
     gain_plane[1, here] = gain_pair[...]
     send_back(CUT1, count)
-    each(1, planes, lambda step: plane_arrival(1, step).wait_recv())
-    gain_out[...] = jnp.sum(gain_plane[1], axis=0)
-
-    def drain(slot):
+    def settle(slot):
+        to, _ = partners(slot, me, count)
         inward(slot, 0).wait_send()
         inward(slot, 1).wait_send()
         outward(slot, 0).wait_send()
-        outward(slot, 1).wait_send()
-
-    each(1, count, drain)
+        home(to, 0).wait_recv()
+
+    each(1, count, settle)
     each(1, planes, lambda step: plane_copy(0, step).wait_send())
-    each(1, planes, lambda step: plane_copy(1, step).wait_send())
 
     @pl.when(speaks)
     def _():
         each(1, count, lambda slot: ring_copy(slot).wait_send())
 
-
-    def collect(slot):
-        to, _ = partners(slot, me, count)
-        home(to, 0).wait_recv()
+    each(1, planes, lambda step: plane_arrival(1, step).wait_recv())
+    gain_out[...] = jnp.sum(gain_plane[1], axis=0)
+    each(1, planes, lambda step: plane_copy(1, step).wait_send())
+    mine.wait()
+
+    def settle_last(slot):
+        to, _ = partners(slot, me, count)
+        outward(slot, 1).wait_send()
         home(to, 1).wait_recv()
 
-    each(1, count, collect)
-    mine.wait()
+    each(1, count, settle_last)
 
 
 def unpack(groups, text_block, dhead, returned, gain_sum, txt_out, img_out, txt_grads, img_grads, gain_grad):

time: 206 us -> 205 us (level)
  no operation moved by 1% of the time
where the time goes in v3:
time: 205 us
  Pallas kernels  205 us (100%)
    pallas_call x1, Pallas kernels, shards(): pl.pallas_call(functools.partial(attend, count, samples, text_block, bloc...  202 us

profile of v3, /device:TPU:1, one launch (start us, length us, event | category | flops | bytes accessed | tf_op | source)
XLA Modules:
  0.0 205.2 jit_solution(2653394863343085290)
XLA Ops:
  0.6 201.8 %attend.1 = (bf16[32,4,64,128]{3,2,1,0:T(8,128)(2,1)}, f32[4,128]{1,0:T(4,128)}) custom-call(bf16[8,3,8,512]{3,2,1,0:T(8,128)(2,1)} %bitcast.5, bf16[8,3,56,512]{3,2,1,0:T(8,128)(2,1)} %bitcast.4, bf16[8,8,512]{2,1,0:T(8,128)(2,1)} %txt_cot_hbm.1, bf16[8,56,512]{2,1,0:T(8,128)(2,1)} %img_cot_hbm.1, s32[8]{0:T(128)} %length_hbm.1, f32[4,128]{1,0:T(4,128)} %gains_hbm.1), custom_call_target="tpu_custom_call" | custom-call | tf_op jit(solution)/shard_map/attend/pallas_call | solution.py:490
  202.5 2.7 %unpack.1 = (bf16[8,8,512]{2,1,0:T(8,128)(2,1)}, bf16[8,56,512]{2,1,0:T(8,128)(2,1)}, bf16[8,3,8,512]{3,2,1,0:T(8,128)(2,1)}, bf16[8,3,56,512]{3,2,1,0:T(8,128)(2,1)}, f32[4,128]{1,0:T(4,128)}) custom-call(bf16[32,4,64,128]{3,2,1,0:T(8,128)(2,1)} %get-tuple-element.12.returned, f32[4,128]{1,0:T(4,128)} %get-tuple-element.13.gain_sum), custom_call_target="tpu_custom_call" | custom-call | tf_op jit(solution)/shard_map/unpack/pallas_call | solution.py:536
